TPU v7x, 32 devices: a whole 2x2x4 slice. The times are simulated.
32 devices in a mesh: chan: 8 (over z, x), freq: 4 (over y, core).
Axes of the slice: x: 2, y: 2, z: 4, core: 2. Of those that a mesh axis runs over, the one named last changes fastest.
Arguments:
- traces: bfloat16 [1024, 20480], P('chan', 'freq'), may hold values from -2000 to 2000
- kept_bins: int32 [128], replicated, may hold values from 1 to 255, as said below
- round_masks: int32 [2], replicated, may hold values from 1 to 7, as said below
Outputs:
- cross_spectra: float32 [2, 128, 2, 1024, 128], P(None, 'freq', None, 'chan')
- auto_spectra: float32 [128, 2, 1024, 128], P('freq', None, 'chan')
Inputs may be any that keep to these rules, and one draw needn't show every extreme that they name: `kept_bins`: 128 distinct bin numbers in increasing order; 1 and 255 are among them. `round_masks`: 2 distinct numbers; in round r channel block b is paired with block b XOR round_masks[r].
All inputs are finite; a program needn't handle non-finite values.
Results may differ from a plain program's by a relative error of at most 0.0066.
Values may be sent and summed in bfloat16 or wider, within the bound.
A program may use at most 64 MiB of HBM per device.

v0:
```python
import functools
import math

import jax
import jax.numpy as jnp
from jax import lax
from jax.experimental import pallas as pl
from jax.experimental.pallas import tpu as pltpu
from jax.sharding import PartitionSpec as P

NS = 512
HOP = NS // 2
EPSILON = 1e-06
PARTS = 2
BINS = 4


def moved(piece, mask):
    route = [(i, i ^ mask) for i in range(lax.axis_size("chan"))]
    return lax.ppermute(piece, "chan", route)


def dft_table(kept_bins):
    sample_index = jnp.arange(NS, dtype=jnp.int32)
    phase_index = kept_bins[:, None] * sample_index[None, :] % NS
    angles = phase_index.astype(jnp.float32) * jnp.float32(2.0 * math.pi / NS)
    hann_taper = 0.5 - 0.5 * jnp.cos(
        sample_index.astype(jnp.float32) * jnp.float32(2.0 * math.pi / NS)
    )
    stacked = jnp.stack([hann_taper * jnp.cos(angles), -hann_taper * jnp.sin(angles)], axis=1)
    return stacked.reshape(kept_bins.shape[0] * 2, NS).astype(jnp.bfloat16)


def nt_dot(a, b):
    return lax.dot_general(a, b, (((1,), (1,)), ((), ())), preferred_element_type=jnp.float32)


def spectra_kernel(frames, ranks, *refs):
    masks_ref, traces_ref, transform_ref, arrived_ref, index_ref = refs[:5]
    rows, sends, following_ref, send_sem, recv_sem, own_sem, edge_sem = refs[5:]
    me = lax.axis_index("freq")
    peers = [lax.rem(me + d, ranks) for d in range(1, ranks)]
    barrier = pltpu.get_barrier_semaphore()
    for peer in peers:
        pl.semaphore_signal(
            barrier, inc=1, device_id={"freq": peer}, device_id_type=pl.DeviceIdType.MESH
        )
    low = jnp.minimum(masks_ref[0], masks_ref[1])
    high = jnp.maximum(masks_ref[0], masks_ref[1])
    before = (low - 1) * (lax.axis_size("chan") - 1) - lax.div(low * (low - 1), 2)
    index_ref[0] = before + high - low - 1
    edge = pltpu.make_async_remote_copy(
        src_ref=traces_ref.at[:, pl.ds(0, HOP)],
        dst_ref=following_ref,
        send_sem=edge_sem.at[0],
        recv_sem=edge_sem.at[1],
        device_id={"freq": lax.rem(me + ranks - 1, ranks)},
        device_id_type=pl.DeviceIdType.MESH,
    )
    count = transform_ref.shape[0]
    for w in range(frames - 1):
        if w == frames // 2:
            pl.semaphore_wait(barrier, ranks - 1)
            edge.start()
        rows[pl.ds(w, count, stride=frames), :] = nt_dot(
            transform_ref[...], traces_ref[:, w * HOP : w * HOP + NS]
        )
    last = nt_dot(transform_ref[:, :HOP], traces_ref[:, (frames - 1) * HOP :])
    edge.wait()
    beyond = nt_dot(transform_ref[:, HOP:], following_ref[...])
    last = last + jnp.where(me < ranks - 1, beyond, 0.0)
    rows[pl.ds(frames - 1, count, stride=frames), :] = last
    length = sends.shape[1]
    for r in range(ranks):
        sends[r] = rows[r * length : (r + 1) * length].astype(jnp.bfloat16)
    copies = [
        pltpu.make_async_remote_copy(
            src_ref=sends.at[peer],
            dst_ref=arrived_ref.at[me],
            send_sem=send_sem.at[i],
            recv_sem=recv_sem.at[i],
            device_id={"freq": peer},
            device_id_type=pl.DeviceIdType.MESH,
        )
        for i, peer in enumerate(peers)
    ]
    copies.append(pltpu.make_async_copy(sends.at[me], arrived_ref.at[me], own_sem))
    for copy in copies:
        copy.start()
    for copy in copies:
        copy.wait()


def spectra_of(masks, traces, transform):
    channels, samples = traces.shape
    frames = samples // HOP
    ranks = lax.axis_size("freq")
    total = transform.shape[0] * frames
    shape = (ranks, total // ranks, channels)
    return pl.pallas_call(
        functools.partial(spectra_kernel, frames, ranks),
        out_shape=[
            jax.ShapeDtypeStruct(shape, jnp.bfloat16),
            jax.ShapeDtypeStruct((1,), jnp.int32),
        ],
        in_specs=[
            pl.BlockSpec(memory_space=pltpu.SMEM),
            pl.BlockSpec(memory_space=pltpu.VMEM),
            pl.BlockSpec(memory_space=pltpu.VMEM),
        ],
        out_specs=[
            pl.BlockSpec(memory_space=pl.ANY),
            pl.BlockSpec(memory_space=pltpu.SMEM),
        ],
        scratch_shapes=[
            pltpu.VMEM((total, channels), jnp.float32),
            pltpu.VMEM(shape, jnp.bfloat16),
            pltpu.VMEM((channels, HOP), jnp.bfloat16),
            pltpu.SemaphoreType.DMA((ranks - 1,)),
            pltpu.SemaphoreType.DMA((ranks - 1,)),
            pltpu.SemaphoreType.DMA,
            pltpu.SemaphoreType.DMA((2,)),
        ],
        compiler_params=pltpu.CompilerParams(
            collective_id=0, has_side_effects=True, vmem_limit_bytes=32 * 2**20
        ),
    )(masks, traces, transform)


def correlate_kernel(frames, windows, masks_ref, *refs):
    cross_ref, auto_ref = refs[-2:]
    span = 2 * frames
    scale = 1.0 / math.sqrt(windows)
    low_first = jnp.where(masks_ref[0] > masks_ref[1], 1, 0)
    blocks = [
        [ref[s].astype(jnp.float32) for ref in refs[at : at + PARTS] for s in range(ref.shape[0])]
        for at in range(0, 3 * PARTS, PARTS)
    ]
    row = lax.broadcasted_iota(jnp.int32, (span, 1), 0)
    sign = jnp.where(row < frames, 1.0, -1.0).astype(jnp.float32)
    for b in range(BINS):
        whitened = []
        for block in blocks:
            values = [part[b * span : (b + 1) * span] for part in block]
            power = sum(jnp.sum(v * v, axis=0, keepdims=True) for v in values) / windows
            gain = lax.rsqrt(power + EPSILON)
            whitened.append([v * gain for v in values])
        left = jnp.concatenate(
            [
                jnp.concatenate([v, pltpu.roll(v, frames, 0) * sign], axis=1)
                for v in whitened[0]
            ],
            axis=0,
        ).astype(jnp.bfloat16)
        right = jnp.concatenate(
            [jnp.concatenate(columns, axis=1) for columns in zip(*whitened)], axis=0
        ).astype(jnp.bfloat16)
        product = scale * lax.dot_general(
            left, right, (((0,), (0,)), ((), ())), preferred_element_type=jnp.float32
        )
        channels = product.shape[0] // 2
        for p in range(2):
            half = product[p * channels : (p + 1) * channels]
            auto_ref[b, p] = half[:, :channels]
            cross_ref[low_first, b, p] = half[:, channels : 2 * channels]
            cross_ref[1 - low_first, b, p] = half[:, 2 * channels :]


def correlate(masks, own, low, high, frames, windows):
    sources, rows, channels = own[0].shape
    span = 2 * frames
    bins = rows // span
    in_spec = pl.BlockSpec((sources, BINS * span, channels), lambda i, masks: (0, i, 0))
    return pl.pallas_call(
        functools.partial(correlate_kernel, frames, windows),
        grid_spec=pltpu.PrefetchScalarGridSpec(
            num_scalar_prefetch=1,
            grid=(bins // BINS,),
            in_specs=[in_spec] * (3 * PARTS),
            out_specs=[
                pl.BlockSpec((2, BINS, 2, channels, channels), lambda i, masks: (0, i, 0, 0, 0)),
                pl.BlockSpec((BINS, 2, channels, channels), lambda i, masks: (i, 0, 0, 0)),
            ],
        ),
        out_shape=[
            jax.ShapeDtypeStruct((2, bins, 2, channels, channels), jnp.float32),
            jax.ShapeDtypeStruct((bins, 2, channels, channels), jnp.float32),
        ],
        compiler_params=pltpu.CompilerParams(vmem_limit_bytes=40 * 2**20),
    )(masks, *own, *low, *high)


def pair_exchange(index, pieces):
    blocks = lax.axis_size("chan")

    def branch(low, high, pieces):
        half = blocks // 2
        if not (low & half and high & half):
            return tuple([moved(piece, mask) for piece in pieces] for mask in (low, high))
        lead = low if low.bit_count() <= high.bit_count() else high
        leading, trailing = [], []
        for piece in pieces:
            if leading:
                piece, leading[-1] = lax.optimization_barrier((piece, leading[-1]))
            leading.append(moved(piece, lead))
            trailing.append(moved(leading[-1], low ^ high))
        return (leading, trailing) if lead == low else (trailing, leading)

    pairs = [(a, b) for a in range(1, blocks) for b in range(a + 1, blocks)]
    return lax.switch(index, [functools.partial(branch, a, b) for a, b in pairs], pieces)


def mask_exchange(mask, pieces):
    blocks = lax.axis_size("chan")
    branches = [
        lambda pieces, m=m: [moved(piece, m) for piece in pieces] for m in range(1, blocks)
    ]
    return lax.switch(mask - 1, branches, pieces)


def body(traces, kept_bins, round_masks):
    frames = traces.shape[1] // HOP
    ranks = lax.axis_size("freq")
    arrived, index = spectra_of(round_masks, traces, dft_table(kept_bins))
    step = ranks // PARTS
    own = tuple(arrived[i * step : (i + 1) * step] for i in range(PARTS))
    if lax.axis_size("chan") <= 8:
        low, high = pair_exchange(index[0], own)
    else:
        low = mask_exchange(jnp.minimum(round_masks[0], round_masks[1]), own)
        high = mask_exchange(jnp.maximum(round_masks[0], round_masks[1]), own)
    cross, auto = correlate(round_masks, own, low, high, frames, frames * ranks)
    return cross, auto


def solution(mesh):
    placed = (P("chan", "freq"), P(), P())
    return jax.shard_map(
        body,
        mesh=mesh,
        in_specs=placed,
        out_specs=(P(None, "freq", None, "chan", None), P("freq", None, "chan", None)),
        check_vma=False,
    )
```

profile of v0, /device:TPU:0, one launch (start us, length us, event | category | flops | bytes accessed | tf_op | source)
XLA Modules:
  0.0 98.0 jit_solution(4232216734945672775)
XLA Ops:
  0.6 0.0 copy-start.1
  0.6 0.0 copy-start
  0.7 2.0 %multiply_convert_fusion.1 = (bf16[128,1,512]{2,0,1:T(8,128)(2,1)S(1)}, bf16[128,1,512]{2,0,1:T(8,128)(2,1)S(1)}) fusion(s32[128]{0:T(128)} %param.25, f32[512]{0:T(512)S(1)} %get-tuple-element.156, f32[512]{0:T(512)S(1)} %get-tuple-element.157), kind=kLoop, calls=%fused_computation.8 | loop fusion | flops 1179648 | bytes 266752 | tf_op jit(solution)/shard_map/convert
  2.7 0.3 copy.5
  3.0 0.1 convert_element_type.31.refs_2_
  3.1 0.0 copy-done.1
  3.1 0.0 copy-done
  3.2 21.2 %shard_map.50 = (bf16[4,1280,128]{2,1,0:T(8,128)(2,1)S(1)}, s32[1]{0:T(128)}) custom-call(s32[2]{0:T(128)S(1)} %copy-done.1, bf16[128,5120]{1,0:T(8,128)(2,1)S(1)} %copy-done, bf16[256,512]{1,0:T(8,128)(2,1)S(1)} %convert_element_type.31.refs_2_), custom_call_target="tpu_custom_call" | custom-call | tf_op jit(solution)/shard_map/pallas_call | solution.py:100
  25.0 0.1 fusion.7
  25.1 62.7 %conditional.1 = (bf16[2,1280,128]{2,1,0:T(8,128)(2,1)}, bf16[2,1280,128]{2,1,0:T(8,128)(2,1)}, bf16[2,1280,128]{2,1,0:T(8,128)(2,1)}, bf16[2,1280,128]{2,1,0:T(8,128)(2,1)}) conditional(s32[]{:T(128)} %bitcast, (bf16[2,1280,128]{2,1,0:T(8,128)(2,1)S(1)}, bf16[2,1280,128]{2,1,0:T(8,128)(2,1)S(1)}) %tuple.97, ...), branch_computations={%region_0.1_spmd, %region_1.2_spmd, %region_2.3_spmd, %region_3.4_... | conditional | bytes 10485952 | solution.py:210
  25.1 4.6 %collective-permute-start.22 = (bf16[2,1280,128]{2,1,0:T(8,128)(2,1)S(1)}, bf16[2,1280,128]{2,1,0:T(8,128)(2,1)}, u32[]{:S(2)}, u32[]{:S(2)}) collective-permute-start(bf16[2,1280,128]{2,1,0:T(8,128)(2,1)S(1)} %get-tuple-element.94), channel_id=1, source_target_pairs={{0,28},{4,24},{8,20},{12,16},{16,12},{20,8},{24,4},{28,0},{1,29},{... | collective-permute-start | bytes 1966088 | tf_op jit(solution)/shard_map/cond/branch_5_fun/ppermute | solution.py:20
  29.7 0.5 collective-permute-start.20
  30.3 1.2 %collective-permute-start.23 = (bf16[2,1280,128]{2,1,0:T(8,128)(2,1)S(1)}, bf16[2,1280,128]{2,1,0:T(8,128)(2,1)}, u32[]{:S(2)}, u32[]{:S(2)}) collective-permute-start(bf16[2,1280,128]{2,1,0:T(8,128)(2,1)S(1)} %get-tuple-element.95), channel_id=1, source_target_pairs={{0,28},{4,24},{8,20},{12,16},{16,12},{20,8},{24,4},{28,0},{1,29},{... | collective-permute-start | bytes 1966088 | tf_op jit(solution)/shard_map/cond/branch_5_fun/ppermute | solution.py:20
  31.4 0.5 collective-permute-start.21
  31.9 13.3 %collective-permute-done.22 = bf16[2,1280,128]{2,1,0:T(8,128)(2,1)} collective-permute-done((bf16[2,1280,128]{2,1,0:T(8,128)(2,1)S(1)}, bf16[2,1280,128]{2,1,0:T(8,128)(2,1)}, u32[]{:S(2)}, u32[]{:S(2)}) %collective-permute-start.22) | collective-permute-done | bytes 655392 | tf_op jit(solution)/shard_map/cond/branch_5_fun/ppermute | solution.py:20
  45.3 28.5 %collective-permute-done.20 = bf16[2,1280,128]{2,1,0:T(8,128)(2,1)} collective-permute-done((bf16[2,1280,128]{2,1,0:T(8,128)(2,1)S(1)}, bf16[2,1280,128]{2,1,0:T(8,128)(2,1)}, u32[]{:S(2)}, u32[]{:S(2)}) %collective-permute-start.20) | collective-permute-done | bytes 655392 | tf_op jit(solution)/shard_map/cond/branch_5_fun/ppermute | solution.py:20
  73.8 0.0 collective-permute-done.23
  73.8 14.0 %collective-permute-done.21 = bf16[2,1280,128]{2,1,0:T(8,128)(2,1)} collective-permute-done((bf16[2,1280,128]{2,1,0:T(8,128)(2,1)S(1)}, bf16[2,1280,128]{2,1,0:T(8,128)(2,1)}, u32[]{:S(2)}, u32[]{:S(2)}) %collective-permute-start.21) | collective-permute-done | bytes 655392 | tf_op jit(solution)/shard_map/cond/branch_5_fun/ppermute | solution.py:20
  87.8 10.2 %shard_map.51 = (f32[2,32,2,128,128]{4,3,2,1,0:T(8,128)}, f32[32,2,128,128]{3,2,1,0:T(8,128)}) custom-call(s32[2]{0:T(128)S(1)} %copy-done.1, bf16[2,1280,128]{2,1,0:T(8,128)(2,1)S(1)} %get-tuple-element.153.refs_0_, bf16[2,1280,128]{2,1,0:T(8,128)(2,1)S(1)} %get-tuple-element.152.refs_1_, bf16[2,1280,128]{2,1,0:T(8,128)(2,1)} %get-tuple-element.148.refs_2_, ...), custom_call_target="tpu_custom_call" | custom-call | tf_op jit(solution)/shard_map/pallas_call | solution.py:174
  (2 shorter events, 0.1 us)
Async XLA Ops:
  0.6 2.5 %copy-start.1 = (s32[2]{0:T(128)S(1)}, s32[2]{0:T(128)}, u32[]{:S(2)}) copy-start(s32[2]{0:T(128)} %masks_ref.1) | copy-start | bytes 28
  0.6 2.5 %copy-start = (bf16[128,5120]{1,0:T(8,128)(2,1)S(1)}, bf16[128,5120]{1,0:T(8,128)(2,1)}, u32[]{:S(2)}) copy-start(bf16[128,5120]{1,0:T(8,128)(2,1)} %refs_1_.1) | copy-start | bytes 3932164
  25.1 20.2 %collective-permute-start.22 = (bf16[2,1280,128]{2,1,0:T(8,128)(2,1)S(1)}, bf16[2,1280,128]{2,1,0:T(8,128)(2,1)}, u32[]{:S(2)}, u32[]{:S(2)}) collective-permute-start(bf16[2,1280,128]{2,1,0:T(8,128)(2,1)S(1)} %get-tuple-element.94), channel_id=1, source_target_pairs={{0,28},{4,24},{8,20},{12,16},{16,12},{20,8},{24,4},{28,0},{1,29},{... | collective-permute-start | bytes 1966088 | tf_op jit(solution)/shard_map/cond/branch_5_fun/ppermute | solution.py:20
  29.7 44.1 %collective-permute-start.20 = (bf16[2,1280,128]{2,1,0:T(8,128)(2,1)S(1)}, bf16[2,1280,128]{2,1,0:T(8,128)(2,1)}, u32[]{:S(2)}, u32[]{:S(2)}) collective-permute-start(bf16[2,1280,128]{2,1,0:T(8,128)(2,1)S(1)} %get-tuple-element.94), channel_id=1, source_target_pairs={{0,4},{4,0},{8,12},{12,8},{16,20},{20,16},{24,28},{28,24},{1,5},{5... | collective-permute-start | bytes 1966088 | tf_op jit(solution)/shard_map/cond/branch_5_fun/ppermute | solution.py:20
  30.3 43.5 %collective-permute-start.23 = (bf16[2,1280,128]{2,1,0:T(8,128)(2,1)S(1)}, bf16[2,1280,128]{2,1,0:T(8,128)(2,1)}, u32[]{:S(2)}, u32[]{:S(2)}) collective-permute-start(bf16[2,1280,128]{2,1,0:T(8,128)(2,1)S(1)} %get-tuple-element.95), channel_id=1, source_target_pairs={{0,28},{4,24},{8,20},{12,16},{16,12},{20,8},{24,4},{28,0},{1,29},{... | collective-permute-start | bytes 1966088 | tf_op jit(solution)/shard_map/cond/branch_5_fun/ppermute | solution.py:20
  31.4 56.4 %collective-permute-start.21 = (bf16[2,1280,128]{2,1,0:T(8,128)(2,1)S(1)}, bf16[2,1280,128]{2,1,0:T(8,128)(2,1)}, u32[]{:S(2)}, u32[]{:S(2)}) collective-permute-start(bf16[2,1280,128]{2,1,0:T(8,128)(2,1)S(1)} %get-tuple-element.95), channel_id=1, source_target_pairs={{0,4},{4,0},{8,12},{12,8},{16,20},{20,16},{24,28},{28,24},{1,5},{5... | collective-permute-start | bytes 1966088 | tf_op jit(solution)/shard_map/cond/branch_5_fun/ppermute | solution.py:20
where the time goes:
time: 98.6 us; the launch traced here: 98 us
  waiting for transfers between devices  55.9 us (57%)
  Pallas kernels  31.4 us (32%)
  starting transfers between devices  6.81 us (7%)
  other arithmetic  2.08 us (2%)
  between operations  1.33 us (1%)
    ppermute x4, waiting for transfers between devices, moved(): return lax.ppermute(piece, 'chan', route)  55.9 us
    pallas_call x1, Pallas kernels, spectra_of(): pl.pallas_call(functools.partial(spectra_kernel, frames, ranks), out_shap...  21.2 us
    pallas_call x1, Pallas kernels, correlate(): pl.pallas_call(functools.partial(correlate_kernel, frames, windows), grid...  10.2 us
    ppermute x4, starting transfers between devices, moved(): return lax.ppermute(piece, 'chan', route)  6.81 us
    another operation x1, other arithmetic  2.01 us
  transfers between devices with their start and end apart: 4, of which 3 were waited for; matrix products, arithmetic and copies ran while one was open for 0% of the time, Pallas kernels for 0%

commit v1 on v0

--- a/solution.py
+++ b/solution.py
@@ -128,13 +128,13 @@
 
 
 def correlate_kernel(frames, windows, masks_ref, *refs):
-    cross_ref, auto_ref = refs[-2:]
+    *refs, out_ref = refs
     span = 2 * frames
     scale = 1.0 / math.sqrt(windows)
     low_first = jnp.where(masks_ref[0] > masks_ref[1], 1, 0)
     blocks = [
         [ref[s].astype(jnp.float32) for ref in refs[at : at + PARTS] for s in range(ref.shape[0])]
-        for at in range(0, 3 * PARTS, PARTS)
+        for at in range(0, len(refs), PARTS)
     ]
     row = lax.broadcasted_iota(jnp.int32, (span, 1), 0)
     sign = jnp.where(row < frames, 1.0, -1.0).astype(jnp.float32)
@@ -153,7 +153,7 @@
             axis=0,
         ).astype(jnp.bfloat16)
         right = jnp.concatenate(
-            [jnp.concatenate(columns, axis=1) for columns in zip(*whitened)], axis=0
+            [jnp.concatenate(columns, axis=1) for columns in zip(*(whitened[1:] or whitened))], axis=0
         ).astype(jnp.bfloat16)
         product = scale * lax.dot_general(
             left, right, (((0,), (0,)), ((), ())), preferred_element_type=jnp.float32
@@ -161,13 +161,17 @@
         channels = product.shape[0] // 2
         for p in range(2):
             half = product[p * channels : (p + 1) * channels]
-            auto_ref[b, p] = half[:, :channels]
-            cross_ref[low_first, b, p] = half[:, channels : 2 * channels]
-            cross_ref[1 - low_first, b, p] = half[:, 2 * channels :]
-
-
-def correlate(masks, own, low, high, frames, windows):
-    sources, rows, channels = own[0].shape
+            if len(whitened) == 1:
+                out_ref[b, p] = half
+            else:
+                out_ref[low_first, b, p] = half[:, :channels]
+                out_ref[1 - low_first, b, p] = half[:, channels:]
+
+
+def correlate(masks, blocks, frames, windows):
+    sources, rows, channels = blocks[0].shape
+    lead = () if len(blocks) == PARTS else (2,)
+    home = (0,) * len(lead)
     span = 2 * frames
     bins = rows // span
     in_spec = pl.BlockSpec((sources, BINS * span, channels), lambda i, masks: (0, i, 0))
@@ -176,27 +180,28 @@
         grid_spec=pltpu.PrefetchScalarGridSpec(
             num_scalar_prefetch=1,
             grid=(bins // BINS,),
-            in_specs=[in_spec] * (3 * PARTS),
-            out_specs=[
-                pl.BlockSpec((2, BINS, 2, channels, channels), lambda i, masks: (0, i, 0, 0, 0)),
-                pl.BlockSpec((BINS, 2, channels, channels), lambda i, masks: (i, 0, 0, 0)),
-            ],
+            in_specs=[in_spec] * len(blocks),
+            out_specs=pl.BlockSpec(
+                (*lead, BINS, 2, channels, channels), lambda i, masks: (*home, i, 0, 0, 0)
+            ),
         ),
-        out_shape=[
-            jax.ShapeDtypeStruct((2, bins, 2, channels, channels), jnp.float32),
-            jax.ShapeDtypeStruct((bins, 2, channels, channels), jnp.float32),
-        ],
+        out_shape=jax.ShapeDtypeStruct((*lead, bins, 2, channels, channels), jnp.float32),
+        cost_estimate=pl.CostEstimate(
+            flops=0, bytes_accessed=16 * bins * channels * channels, transcendentals=0
+        ),
         compiler_params=pltpu.CompilerParams(vmem_limit_bytes=40 * 2**20),
-    )(masks, *own, *low, *high)
-
-
-def pair_exchange(index, pieces):
+    )(masks, *blocks)
+
+
+def pair_exchange(index, masks, frames, windows, pieces):
     blocks = lax.axis_size("chan")
 
     def branch(low, high, pieces):
         half = blocks // 2
+        auto = correlate(masks, pieces, frames, windows)
         if not (low & half and high & half):
-            return tuple([moved(piece, mask) for piece in pieces] for mask in (low, high))
+            far = [[moved(piece, mask) for piece in pieces] for mask in (low, high)]
+            return (*far, auto)
         lead = low if low.bit_count() <= high.bit_count() else high
         leading, trailing = [], []
         for piece in pieces:
@@ -204,7 +209,8 @@
                 piece, leading[-1] = lax.optimization_barrier((piece, leading[-1]))
             leading.append(moved(piece, lead))
             trailing.append(moved(leading[-1], low ^ high))
-        return (leading, trailing) if lead == low else (trailing, leading)
+        far = (leading, trailing) if lead == low else (trailing, leading)
+        return (*far, auto)
 
     pairs = [(a, b) for a in range(1, blocks) for b in range(a + 1, blocks)]
     return lax.switch(index, [functools.partial(branch, a, b) for a, b in pairs], pieces)
@@ -224,12 +230,14 @@
     arrived, index = spectra_of(round_masks, traces, dft_table(kept_bins))
     step = ranks // PARTS
     own = tuple(arrived[i * step : (i + 1) * step] for i in range(PARTS))
+    windows = frames * ranks
     if lax.axis_size("chan") <= 8:
-        low, high = pair_exchange(index[0], own)
+        low, high, auto = pair_exchange(index[0], round_masks, frames, windows, own)
     else:
         low = mask_exchange(jnp.minimum(round_masks[0], round_masks[1]), own)
         high = mask_exchange(jnp.maximum(round_masks[0], round_masks[1]), own)
-    cross, auto = correlate(round_masks, own, low, high, frames, frames * ranks)
+        auto = correlate(round_masks, own, frames, windows)
+    cross = correlate(round_masks, (*own, *low, *high), frames, windows)
     return cross, auto
 
 

time: 98.6 us -> 99.6 us (1.010)
  waiting for transfers between devices: 55.9 us -> 52.2 us
  Pallas kernels: 31.4 us -> 34.8 us
  local copies, waits for them, and re-layouts: 0.47 us -> 1.78 us
    ppermute x4, waiting for transfers between devices: 55.9 us -> 52.2 us  [moved(): return lax.ppermute(piece, 'chan', route)]
    pallas_call x1 -> x2, Pallas kernels: 10.2 us -> 13.4 us  [correlate(): pl.pallas_call(functools.partial(correlate_kernel, frames, windows), grid...]
    unnamed x4 -> x6, local copies, waits for them, and re-layouts: 0.01 us -> 1.32 us
  transfers between devices with their start and end apart: 4 -> 4, of which waited for: 3 -> 3; matrix products, arithmetic and copies ran while one was open for 0% -> 0% of each run, Pallas kernels for 0% -> 4%
where the time goes in v1:
time: 99.6 us; the launch traced here: 98.9 us
  waiting for transfers between devices  52.2 us (52%)
  Pallas kernels  34.8 us (35%)
  starting transfers between devices  6.81 us (7%)
  other arithmetic  1.99 us (2%)
  local copies, waits for them, and re-layouts  1.78 us (2%)
  between operations  1.39 us (1%)
    ppermute x4, waiting for transfers between devices, moved(): return lax.ppermute(piece, 'chan', route)  52.2 us
    pallas_call x1, Pallas kernels, spectra_of(): pl.pallas_call(functools.partial(spectra_kernel, frames, ranks), out_shap...  21.3 us
    pallas_call x2, Pallas kernels, correlate(): pl.pallas_call(functools.partial(correlate_kernel, frames, windows), grid...  13.4 us
    ppermute x4, starting transfers between devices, moved(): return lax.ppermute(piece, 'chan', route)  6.81 us
  transfers between devices with their start and end apart: 4, of which 3 were waited for; matrix products, arithmetic and copies ran while one was open for 0% of the time, Pallas kernels for 4%

profile of v1, /device:TPU:0, one launch (start us, length us, event | category | flops | bytes accessed | tf_op | source)
XLA Modules:
  0.0 98.9 jit_solution(17305295468786111054)
XLA Ops:
  0.6 0.0 copy-start.2
  0.7 1.9 %multiply_convert_fusion.1 = (bf16[128,1,512]{2,0,1:T(8,128)(2,1)S(1)}, bf16[128,1,512]{2,0,1:T(8,128)(2,1)S(1)}) fusion(s32[128]{0:T(128)} %param.25, f32[512]{0:T(512)S(1)} %get-tuple-element.221, f32[512]{0:T(512)S(1)} %get-tuple-element.222), kind=kLoop, calls=%fused_computation.8 | loop fusion | flops 1179648 | bytes 266752 | tf_op jit(solution)/shard_map/convert
  2.6 0.3 copy.5
  2.9 0.1 convert_element_type.31.refs_2_
  3.0 0.0 copy-start
  3.0 1.3 %copy-done = bf16[128,5120]{1,0:T(8,128)(2,1)S(1)} copy-done((bf16[128,5120]{1,0:T(8,128)(2,1)S(1)}, bf16[128,5120]{1,0:T(8,128)(2,1)}, u32[]{:S(2)}) %copy-start) | copy-done | bytes 1310744
  4.4 21.3 %shard_map.50 = (bf16[4,1280,128]{2,1,0:T(8,128)(2,1)S(1)}, s32[1]{0:T(128)}) custom-call(s32[2]{0:T(128)} %masks_ref.1, bf16[128,5120]{1,0:T(8,128)(2,1)S(1)} %copy-done, bf16[256,512]{1,0:T(8,128)(2,1)S(1)} %convert_element_type.31.refs_2_), custom_call_target="tpu_custom_call" | custom-call | tf_op jit(solution)/shard_map/pallas_call | solution.py:100
  26.4 0.1 fusion.7
  26.5 0.0 copy-done.2
  26.5 62.7 %conditional.1 = (bf16[2,1280,128]{2,1,0:T(8,128)(2,1)}, bf16[2,1280,128]{2,1,0:T(8,128)(2,1)}, bf16[2,1280,128]{2,1,0:T(8,128)(2,1)}, bf16[2,1280,128]{2,1,0:T(8,128)(2,1)}, f32[32,2,128,128]{3,2,1,0:T(8,128)S(1)}) conditional(s32[]{:T(128)} %bitcast, (bf16[2,1280,128]{2,1,0:T(8,128)(2,1)S(1)}, ...), branch_computations={%region_0.1_spmd, %region_1.2_spmd, %region_2.3_spmd, %region_3.4_... | conditional | bytes 18874568 | solution.py:216
  26.5 4.6 %collective-permute-start.22 = (bf16[2,1280,128]{2,1,0:T(8,128)(2,1)S(1)}, bf16[2,1280,128]{2,1,0:T(8,128)(2,1)}, u32[]{:S(2)}, u32[]{:S(2)}) collective-permute-start(bf16[2,1280,128]{2,1,0:T(8,128)(2,1)S(1)} %get-tuple-element.141.refs_0_), channel_id=1, source_target_pairs={{0,28},{4,24},{8,20},{12,16},{16,12},{20,8},{24,4},{28,0},{1,29},{... | collective-permute-start | bytes 1966088 | tf_op jit(solution)/shard_map/cond/branch_5_fun/ppermute | solution.py:20
  31.1 0.5 collective-permute-start.20
  31.7 1.2 %collective-permute-start.23 = (bf16[2,1280,128]{2,1,0:T(8,128)(2,1)S(1)}, bf16[2,1280,128]{2,1,0:T(8,128)(2,1)}, u32[]{:S(2)}, u32[]{:S(2)}) collective-permute-start(bf16[2,1280,128]{2,1,0:T(8,128)(2,1)S(1)} %get-tuple-element.142.refs_1_), channel_id=1, source_target_pairs={{0,28},{4,24},{8,20},{12,16},{16,12},{20,8},{24,4},{28,0},{1,29},{... | collective-permute-start | bytes 1966088 | tf_op jit(solution)/shard_map/cond/branch_5_fun/ppermute | solution.py:20
  32.8 0.5 collective-permute-start.21
  33.3 3.7 %branch_5_fun.1 = f32[32,2,128,128]{3,2,1,0:T(8,128)S(1)} custom-call(s32[2]{0:T(128)S(1)} %get-tuple-element.143.masks_ref, bf16[2,1280,128]{2,1,0:T(8,128)(2,1)S(1)} %get-tuple-element.141.refs_0_, bf16[2,1280,128]{2,1,0:T(8,128)(2,1)S(1)} %get-tuple-element.142.refs_1_), custom_call_target="tpu_custom_call" | custom-call | bytes 8388608 | tf_op jit(solution)/shard_map/cond/branch_5_fun/pallas_call | solution.py:178
  37.1 9.6 %collective-permute-done.22 = bf16[2,1280,128]{2,1,0:T(8,128)(2,1)} collective-permute-done((bf16[2,1280,128]{2,1,0:T(8,128)(2,1)S(1)}, bf16[2,1280,128]{2,1,0:T(8,128)(2,1)}, u32[]{:S(2)}, u32[]{:S(2)}) %collective-permute-start.22) | collective-permute-done | bytes 655392 | tf_op jit(solution)/shard_map/cond/branch_5_fun/ppermute | solution.py:20
  46.7 28.5 %collective-permute-done.20 = bf16[2,1280,128]{2,1,0:T(8,128)(2,1)} collective-permute-done((bf16[2,1280,128]{2,1,0:T(8,128)(2,1)S(1)}, bf16[2,1280,128]{2,1,0:T(8,128)(2,1)}, u32[]{:S(2)}, u32[]{:S(2)}) %collective-permute-start.20) | collective-permute-done | bytes 655392 | tf_op jit(solution)/shard_map/cond/branch_5_fun/ppermute | solution.py:20
  75.2 0.0 collective-permute-done.23
  75.2 14.0 %collective-permute-done.21 = bf16[2,1280,128]{2,1,0:T(8,128)(2,1)} collective-permute-done((bf16[2,1280,128]{2,1,0:T(8,128)(2,1)S(1)}, bf16[2,1280,128]{2,1,0:T(8,128)(2,1)}, u32[]{:S(2)}, u32[]{:S(2)}) %collective-permute-start.21) | collective-permute-done | bytes 655392 | tf_op jit(solution)/shard_map/cond/branch_5_fun/ppermute | solution.py:20
  89.2 0.0 copy-start.1
  89.2 9.7 %shard_map.51 = f32[2,32,2,128,128]{4,3,2,1,0:T(8,128)} custom-call(s32[2]{0:T(128)S(1)} %copy-done.2, bf16[2,1280,128]{2,1,0:T(8,128)(2,1)S(1)} %get-tuple-element.218.refs_0_, bf16[2,1280,128]{2,1,0:T(8,128)(2,1)S(1)} %get-tuple-element.217.refs_1_, bf16[2,1280,128]{2,1,0:T(8,128)(2,1)} %get-tuple-element.212.refs_2_, ...), custom_call_target="tpu_custom_call" | custom-call | bytes 8388608 | tf_op jit(solution)/shard_map/pallas_call | solution.py:178
  98.9 0.0 copy-done.1
  (2 shorter events, 0.1 us)
Async XLA Ops:
  0.6 25.9 %copy-start.2 = (s32[2]{0:T(128)S(1)}, s32[2]{0:T(128)}, u32[]{:S(2)}) copy-start(s32[2]{0:T(128)} %masks_ref.1) | copy-start | bytes 28
  3.0 1.3 %copy-start = (bf16[128,5120]{1,0:T(8,128)(2,1)S(1)}, bf16[128,5120]{1,0:T(8,128)(2,1)}, u32[]{:S(2)}) copy-start(bf16[128,5120]{1,0:T(8,128)(2,1)} %refs_1_.1) | copy-start | bytes 3932164
  26.5 20.2 %collective-permute-start.22 = (bf16[2,1280,128]{2,1,0:T(8,128)(2,1)S(1)}, bf16[2,1280,128]{2,1,0:T(8,128)(2,1)}, u32[]{:S(2)}, u32[]{:S(2)}) collective-permute-start(bf16[2,1280,128]{2,1,0:T(8,128)(2,1)S(1)} %get-tuple-element.141.refs_0_), channel_id=1, source_target_pairs={{0,28},{4,24},{8,20},{12,16},{16,12},{20,8},{24,4},{28,0},{1,29},{... | collective-permute-start | bytes 1966088 | tf_op jit(solution)/shard_map/cond/branch_5_fun/ppermute | solution.py:20
  31.1 44.1 %collective-permute-start.20 = (bf16[2,1280,128]{2,1,0:T(8,128)(2,1)S(1)}, bf16[2,1280,128]{2,1,0:T(8,128)(2,1)}, u32[]{:S(2)}, u32[]{:S(2)}) collective-permute-start(bf16[2,1280,128]{2,1,0:T(8,128)(2,1)S(1)} %get-tuple-element.141.refs_0_), channel_id=1, source_target_pairs={{0,4},{4,0},{8,12},{12,8},{16,20},{20,16},{24,28},{28,24},{1,5},{5... | collective-permute-start | bytes 1966088 | tf_op jit(solution)/shard_map/cond/branch_5_fun/ppermute | solution.py:20
  31.7 43.5 %collective-permute-start.23 = (bf16[2,1280,128]{2,1,0:T(8,128)(2,1)S(1)}, bf16[2,1280,128]{2,1,0:T(8,128)(2,1)}, u32[]{:S(2)}, u32[]{:S(2)}) collective-permute-start(bf16[2,1280,128]{2,1,0:T(8,128)(2,1)S(1)} %get-tuple-element.142.refs_1_), channel_id=1, source_target_pairs={{0,28},{4,24},{8,20},{12,16},{16,12},{20,8},{24,4},{28,0},{1,29},{... | collective-permute-start | bytes 1966088 | tf_op jit(solution)/shard_map/cond/branch_5_fun/ppermute | solution.py:20
  32.8 56.4 %collective-permute-start.21 = (bf16[2,1280,128]{2,1,0:T(8,128)(2,1)S(1)}, bf16[2,1280,128]{2,1,0:T(8,128)(2,1)}, u32[]{:S(2)}, u32[]{:S(2)}) collective-permute-start(bf16[2,1280,128]{2,1,0:T(8,128)(2,1)S(1)} %get-tuple-element.142.refs_1_), channel_id=1, source_target_pairs={{0,4},{4,0},{8,12},{12,8},{16,20},{20,16},{24,28},{28,24},{1,5},{5... | collective-permute-start | bytes 1966088 | tf_op jit(solution)/shard_map/cond/branch_5_fun/ppermute | solution.py:20
  89.2 9.7 %copy-start.1 = (f32[32,2,128,128]{3,2,1,0:T(8,128)}, f32[32,2,128,128]{3,2,1,0:T(8,128)S(1)}, u32[]{:S(2)}) copy-start(f32[32,2,128,128]{3,2,1,0:T(8,128)S(1)} %get-tuple-element.209) | copy-start | bytes 12582916
